TPU v7x, 32 devices: a whole 2x2x4 slice. The times are simulated.
32 devices in a mesh: ctx: 4 (over x, core), fsdp: 8 (over z, y).
Axes of the slice: x: 2, y: 2, z: 4, core: 2. Of those that a mesh axis runs over, the one named last changes fastest.
Arguments:
- inputs: bfloat16 [8, 512, 2048], P('fsdp', 'ctx'), may hold values from -6 to 6
- doc_starts: int32 [8, 512], P('fsdp'), may hold values from 0 to 1, as said below
- routes: int32 [8, 512, 8], P('fsdp', 'ctx'), may hold values from 0 to 23, all different within a row; in each aligned block of 128 rows (0 to 127, 128 to 255, ..., all dimensions but the last counted through in order) at most 53 rows name the same one
- gate_weights: float32 [8, 512, 8], P('fsdp', 'ctx'), may hold values from 0.04 to 0.25
- qkv_w: bfloat16 [2048, 3, 2048], P('fsdp'), may hold values from -0.125 to 0.125
- out_w: bfloat16 [2048, 2048], P('fsdp'), may hold values from -2 to 2
- norm_gains: bfloat16 [2048, 2], P('fsdp'), may hold values from 0.5 to 1.5
- head_gains: bfloat16 [128, 2], P('fsdp'), may hold values from 0.5 to 1.5
- gate_up: bfloat16 [2048, 24, 2048], P('ctx', 'fsdp'), may hold values from -0.125 to 0.125
- down_t: bfloat16 [2048, 24, 1024], P('ctx', 'fsdp'), may hold values from -0.75 to 0.75
- cotangent: bfloat16 [8, 512, 2048], P('fsdp', 'ctx'), may hold values from -6 to 6
Outputs:
- block_out: bfloat16 [8, 512, 2048], P('fsdp', 'ctx')
- inputs_grad: float32 [8, 512, 2048], P('fsdp', 'ctx')
- qkv_w_grad: float32 [2048, 3, 2048], P('fsdp')
- out_w_grad: float32 [2048, 2048], P('fsdp')
- norm_gains_grad: float32 [2048, 2], P('fsdp')
- head_gains_grad: float32 [128, 2], P('fsdp')
- gate_up_grad: float32 [2048, 24, 2048], P('ctx', 'fsdp')
- down_t_grad: float32 [2048, 24, 1024], P('ctx', 'fsdp')
Inputs may be any that keep to these rules, and one draw needn't show every extreme that they name: `doc_starts`: 1 marks the first position of a document; position 0 of every stream is 1. `routes`: each row names 8 different experts; in the rows of one device no expert is named more than 53 times, a bound that some block reaches.
All inputs are finite; a program needn't handle non-finite values.
Results may differ from a plain program's by a relative error of at most 0.02.
Values may be sent and summed in bfloat16 or wider, within the bound.
No kernel may reach another device: no remote copies, remote signals or barrier semaphores. Data moves between devices by JAX's collectives and lax.ppermute only.
A program may use at most 384 MiB of HBM per device.

v0:
```python
import math
import jax
import jax.numpy as jnp
from jax import lax
from jax.sharding import PartitionSpec as P

EPS = 1e-06
ROPE_BASE = 10000.0
NEG_FILL = -1e30


def rms_scale(values, gain):
    return values * lax.rsqrt(jnp.mean(values * values, axis=-1, keepdims=True) + EPS) * gain


def rotate(values, cosine, sine_part):
    half_dim = values.shape[-1] // 2
    first = values[..., :half_dim]
    second = values[..., half_dim:]
    return jnp.concatenate(
        [first * cosine - second * sine_part, second * cosine + first * sine_part], axis=-1
    )


def body(
    inputs,
    doc_starts,
    routes,
    gate_weights,
    qkv_w,
    out_w,
    norm_gains,
    head_gains,
    gate_up,
    down_t,
    cotangent,
):
    tok_rows = inputs.shape[1]
    model_width = inputs.shape[2]
    head_dim = head_gains.shape[0] * lax.axis_size("fsdp")
    head_count = model_width // head_dim
    half_dim = head_dim // 2
    score_scale = head_dim ** (-0.5)
    top_count = routes.shape[2]
    hidden_units = down_t.shape[2]
    local_experts = gate_up.shape[1]
    experts_all = local_experts * lax.axis_size("fsdp")
    capacity = tok_rows * top_count * 5 // (experts_all * 4)
    stream_len = doc_starts.shape[1]
    key_width = min(512, stream_len)
    key_count = stream_len // key_width
    position = lax.axis_index("ctx") * tok_rows
    f32 = jnp.float32
    bf16 = jnp.bfloat16
    places = jnp.arange(stream_len, dtype=jnp.int32)
    starts = doc_starts[0]
    begins = lax.cummax(jnp.where(starts == 1, places, jnp.zeros_like(places)), axis=0)
    doc_ids = jnp.cumsum(starts)
    relative = places - begins
    local_docs = lax.dynamic_slice_in_dim(doc_ids, position, tok_rows)
    local_rel = lax.dynamic_slice_in_dim(relative, position, tok_rows)
    key_docs = doc_ids.reshape(key_count, key_width)
    frequency = jnp.exp(jnp.arange(half_dim, dtype=f32) * (-2.0 / head_dim) * math.log(ROPE_BASE))
    angles = local_rel.astype(f32)[:, None] * frequency[None, :]
    cosine = jnp.cos(angles)[:, None, :]
    sine_part = jnp.sin(angles)[:, None, :]
    qkv_full, out_full, norm_full, head_full = (
        lax.all_gather(qkv_w, "fsdp", axis=0, tiled=True),
        lax.all_gather(out_w, "fsdp", axis=0, tiled=True),
        lax.all_gather(norm_gains, "fsdp", axis=0, tiled=True),
        lax.all_gather(head_gains, "fsdp", axis=0, tiled=True),
    )
    x_rows = inputs[0].astype(f32)
    cot_rows = cotangent[0].astype(f32)
    a1_f32, norm_one_back = jax.vjp(rms_scale, x_rows, norm_full[:, 0].astype(f32))
    a1_low = a1_f32.astype(bf16)
    proj = jnp.einsum("td,djk->tjk", a1_low, qkv_full, preferred_element_type=f32)

    def prepare(q_flat, k_flat, q_gain, k_gain):
        q_heads = rms_scale(q_flat.reshape(tok_rows, head_count, head_dim), q_gain)
        k_heads = rms_scale(k_flat.reshape(tok_rows, head_count, head_dim), k_gain)
        return (rotate(q_heads, cosine, sine_part), rotate(k_heads, cosine, sine_part))

    (q_rot, k_rot), prepare_back = jax.vjp(
        prepare, proj[:, 0], proj[:, 1], head_full[:, 0].astype(f32), head_full[:, 1].astype(f32)
    )
    q_low = q_rot.astype(bf16)
    k_low = k_rot.reshape(tok_rows, model_width).astype(bf16)
    v_low = proj[:, 2].astype(bf16)
    keys_all, values_all = (
        lax.all_gather(k_low, "ctx", axis=0, tiled=True),
        lax.all_gather(v_low, "ctx", axis=0, tiled=True),
    )
    key_blocks = keys_all.reshape(key_count, key_width, head_count, head_dim)
    value_blocks = values_all.reshape(key_count, key_width, head_count, head_dim)

    def block_logits(key_block, doc_block):
        logits = (
            jnp.einsum("qhd,khd->hqk", q_low, key_block, preferred_element_type=f32) * score_scale
        )
        same_doc = (local_docs[:, None] == doc_block[None, :])[None]
        return jnp.where(same_doc, logits, NEG_FILL)

    def max_step(running, pieces):
        row_max, summed = running
        key_block, doc_block = pieces
        logits = block_logits(key_block, doc_block)
        new_max = jnp.maximum(row_max, jnp.max(logits, axis=2))
        summed = summed * jnp.exp(row_max - new_max) + jnp.sum(
            jnp.exp(logits - new_max[:, :, None]), axis=2
        )
        return ((new_max, summed), None)

    start_max = jnp.full((head_count, tok_rows), NEG_FILL, f32)
    (row_max, summed), _ = lax.scan(
        max_step, (start_max, jnp.zeros((head_count, tok_rows), f32)), (key_blocks, key_docs)
    )
    log_total = row_max + jnp.log(summed)

    def value_step(attn_acc, pieces):
        key_block, value_block, doc_block = pieces
        attn_probs = jnp.exp(block_logits(key_block, doc_block) - log_total[:, :, None])
        return (
            attn_acc
            + jnp.einsum(
                "hqk,khd->qhd", attn_probs.astype(bf16), value_block, preferred_element_type=f32
            ),
            None,
        )

    attn_acc, _ = lax.scan(
        value_step,
        jnp.zeros((tok_rows, head_count, head_dim), f32),
        (key_blocks, value_blocks, key_docs),
    )
    attn_low = attn_acc.reshape(tok_rows, model_width).astype(bf16)
    h_one = x_rows + jnp.dot(attn_low, out_full, preferred_element_type=f32)
    a2_f32, norm_two_back = jax.vjp(rms_scale, h_one, norm_full[:, 1].astype(f32))
    a2_low = a2_f32.astype(bf16)
    flat_routes = routes[0].reshape(tok_rows * top_count)
    onehot = (flat_routes[:, None] == jnp.arange(experts_all, dtype=jnp.int32)[None, :]).astype(
        jnp.int32
    )
    earlier = jnp.cumsum(onehot, axis=0) - onehot
    slot_in = jnp.sum(earlier * onehot, axis=1)
    slot_index = flat_routes * capacity + slot_in
    token_of = jnp.arange(tok_rows * top_count, dtype=jnp.int32) // top_count
    send_rows = (
        jnp.zeros((experts_all * capacity, model_width), bf16).at[slot_index].set(a2_low[token_of])
    )
    scaled = (
        (gate_weights[0][:, :, None] * cot_rows[:, None, :])
        .reshape(tok_rows * top_count, model_width)
        .astype(bf16)
    )
    send_grads = jnp.zeros((experts_all * capacity, model_width), bf16).at[slot_index].set(scaled)
    got_rows, got_grads = (
        lax.all_to_all(
            send_rows.reshape(experts_all, capacity, model_width),
            "fsdp",
            split_axis=0,
            concat_axis=1,
            tiled=True,
        ),
        lax.all_to_all(
            send_grads.reshape(experts_all, capacity, model_width),
            "fsdp",
            split_axis=0,
            concat_axis=1,
            tiled=True,
        ),
    )
    segment = lax.all_gather(gate_up, "ctx", axis=0, tiled=True)
    gate_add = jnp.einsum(
        "erd,dek->erk", got_rows, segment[:, :, :hidden_units], preferred_element_type=f32
    )
    up_add = jnp.einsum(
        "erd,dek->erk", got_rows, segment[:, :, hidden_units:], preferred_element_type=f32
    )
    sigmoid_g = jax.nn.sigmoid(gate_add)
    activated = gate_add * sigmoid_g
    hidden_low = (activated * up_add).astype(bf16)
    segment = lax.all_gather(down_t, "ctx", axis=0, tiled=True)
    made_block = jnp.einsum("erf,def->erd", hidden_low, segment, preferred_element_type=f32).astype(
        bf16
    )
    made_rows = made_block
    hidden_grad = jnp.einsum("erd,def->erf", got_grads, segment, preferred_element_type=f32)
    made_rows, hidden_grad = (made_rows, hidden_grad)
    gate_grad_low = (
        hidden_grad * up_add * sigmoid_g * (1.0 + gate_add * (1.0 - sigmoid_g))
    ).astype(bf16)
    up_grad_low = (hidden_grad * activated).astype(bf16)
    segment = lax.all_gather(gate_up, "ctx", axis=0, tiled=True)
    part_gate = jnp.einsum(
        "erk,dek->erd", gate_grad_low, segment[:, :, :hidden_units], preferred_element_type=f32
    )
    part_up = jnp.einsum(
        "erk,dek->erd", up_grad_low, segment[:, :, hidden_units:], preferred_element_type=f32
    )
    input_grads = (part_gate + part_up).astype(bf16)
    expert_sums = lax.psum_scatter(
        jnp.concatenate(
            [
                jnp.einsum("erd,erk->dek", got_rows, gate_grad_low, preferred_element_type=f32),
                jnp.einsum("erd,erk->dek", got_rows, up_grad_low, preferred_element_type=f32),
                jnp.einsum("erd,erf->def", got_grads, hidden_low, preferred_element_type=f32),
            ],
            axis=2,
        ).astype(jnp.bfloat16),
        "ctx",
        scatter_dimension=0,
        tiled=True,
    ).astype(jnp.float32)
    back_out, back_in = (
        lax.all_to_all(made_rows, "fsdp", split_axis=1, concat_axis=0, tiled=True),
        lax.all_to_all(input_grads, "fsdp", split_axis=1, concat_axis=0, tiled=True),
    )
    out_rows = back_out.reshape(experts_all * capacity, model_width)[slot_index].reshape(
        tok_rows, top_count, model_width
    )
    mixed = jnp.sum(gate_weights[0][:, :, None] * out_rows.astype(f32), axis=1)
    block_out = (h_one + mixed).astype(bf16)
    in_rows = back_in.reshape(experts_all * capacity, model_width)[slot_index].reshape(
        tok_rows, top_count, model_width
    )
    da2 = jnp.sum(in_rows.astype(f32), axis=1)
    dh_part, gain_two_grad = norm_two_back(da2)
    dh_one = cot_rows + dh_part
    dattn = dh_one.astype(bf16)
    out_grad_low = (
        jnp.einsum("tk,dk->td", dattn, out_full, preferred_element_type=f32)
        .astype(bf16)
        .reshape(tok_rows, head_count, head_dim)
    )
    row_delta = jnp.einsum("qhd,qhd->hq", out_grad_low.astype(f32), attn_acc)

    def grad_step(query_grad, pieces):
        key_block, value_block, doc_block = pieces
        attn_probs = jnp.exp(block_logits(key_block, doc_block) - log_total[:, :, None])
        prob_grad = jnp.einsum(
            "qhd,khd->hqk", out_grad_low, value_block, preferred_element_type=f32
        )
        logit_grad = (attn_probs * (prob_grad - row_delta[:, :, None])).astype(bf16)
        query_grad = (
            query_grad
            + jnp.einsum("hqk,khd->qhd", logit_grad, key_block, preferred_element_type=f32)
            * score_scale
        )
        key_grad = (
            jnp.einsum("hqk,qhd->khd", logit_grad, q_low, preferred_element_type=f32) * score_scale
        )
        value_grad = jnp.einsum(
            "hqk,qhd->khd", attn_probs.astype(bf16), out_grad_low, preferred_element_type=f32
        )
        return (query_grad, (key_grad, value_grad))

    query_grad, (key_grads, value_grads) = lax.scan(
        grad_step,
        jnp.zeros((tok_rows, head_count, head_dim), f32),
        (key_blocks, value_blocks, key_docs),
    )
    key_sum, value_sum = (
        lax.psum_scatter(
            key_grads.reshape(stream_len, model_width).astype(jnp.bfloat16),
            "ctx",
            scatter_dimension=0,
            tiled=True,
        ).astype(jnp.float32),
        lax.psum_scatter(
            value_grads.reshape(stream_len, model_width).astype(jnp.bfloat16),
            "ctx",
            scatter_dimension=0,
            tiled=True,
        ).astype(jnp.float32),
    )
    key_low = key_sum.astype(bf16).astype(f32).reshape(tok_rows, head_count, head_dim)
    query_low = query_grad.astype(bf16).astype(f32)
    dq_proj, dk_proj, q_gain_grad, k_gain_grad = prepare_back((query_low, key_low))
    proj_grad = jnp.stack([dq_proj, dk_proj, value_sum], axis=1).astype(bf16)
    da1 = jnp.einsum("tjk,djk->td", proj_grad, qkv_full, preferred_element_type=f32)
    dx_part, gain_one_grad = norm_one_back(da1)
    inputs_grad = dh_one + dx_part
    projections = jnp.einsum("td,tjk->djk", a1_low, proj_grad, preferred_element_type=f32)
    output_part = jnp.einsum("td,tk->dk", attn_low, dattn, preferred_element_type=f32)
    attn_shard = lax.psum_scatter(
        jnp.concatenate([projections, output_part[:, None, :]], axis=1).astype(jnp.bfloat16),
        "fsdp",
        scatter_dimension=0,
        tiled=True,
    )
    norm_part = jnp.stack([gain_one_grad, gain_two_grad], axis=1)
    head_part = jnp.stack([q_gain_grad, k_gain_grad], axis=1)
    norm_shard, head_shard = (
        lax.psum_scatter(norm_part, "fsdp", scatter_dimension=0, tiled=True),
        lax.psum_scatter(head_part, "fsdp", scatter_dimension=0, tiled=True),
    )
    totals = (
        lax.psum(attn_shard, "ctx").astype(jnp.float32),
        lax.psum(norm_shard.astype(jnp.bfloat16), "ctx").astype(jnp.float32),
        lax.psum(head_shard.astype(jnp.bfloat16), "ctx").astype(jnp.float32),
    )
    return (
        block_out[None],
        inputs_grad[None],
        totals[0][:, :3, :],
        totals[0][:, 3, :],
        totals[1],
        totals[2],
        expert_sums[:, :, : 2 * hidden_units],
        expert_sums[:, :, 2 * hidden_units :],
    )


def solution(mesh):
    return jax.shard_map(
        body,
        mesh=mesh,
        in_specs=(
            P("fsdp", "ctx", None),
            P("fsdp", None),
            P("fsdp", "ctx", None),
            P("fsdp", "ctx", None),
            P("fsdp", None, None),
            P("fsdp", None),
            P("fsdp", None),
            P("fsdp", None),
            P("ctx", "fsdp", None),
            P("ctx", "fsdp", None),
            P("fsdp", "ctx", None),
        ),
        out_specs=(
            P("fsdp", "ctx", None),
            P("fsdp", "ctx", None),
            P("fsdp", None, None),
            P("fsdp", None),
            P("fsdp", None),
            P("fsdp", None),
            P("ctx", "fsdp", None),
            P("ctx", "fsdp", None),
        ),
        check_vma=False,
    )
```

profile of v0, /device:TPU:0, one launch (start us, length us, event | category | flops | bytes accessed | tf_op | source)
XLA Modules:
  0.0 2599.0 jit_solution(13533799499513804395)
XLA Ops:
  7.9 50.7 %all_gather.25 = bf16[2048,2]{0,1:T(2,128)(2,1)S(1)} all-gather(bf16[256,2]{0,1:T(2,128)(2,1)} %param.17), channel_id=1, replica_groups=mesh['ctx'=4,'fsdp'=8] {'fsdp'}, dimensions={0}, use_global_device_ids=true | all-gather | bytes 9216 | tf_op jit(solution)/shard_map/all_gather | solution.py:70
  60.5 432.3 %all-gather.9.cloned.1.call-done = bf16[2048,3,2048]{2,0,1:T(8,128)(2,1)} async-done(((bf16[256,3,2048]{2,0,1:T(8,128)(2,1)}), bf16[2048,3,2048]{2,0,1:T(8,128)(2,1)}) %all-gather.9.cloned.1.call-update) | async-done | bytes 25165840 | tf_op jit(solution)/shard_map/all_gather | solution.py:68
  504.5 19.2 all-gather.1
  575.0 207.0 %all-gather.13.cloned.1.call-done = bf16[2048,2048]{1,0:T(8,128)(2,1)} async-done(((bf16[256,2048]{1,0:T(8,128)(2,1)}), bf16[2048,2048]{1,0:T(8,128)(2,1)}) %all-gather.13.cloned.1.call-update) | async-done | bytes 8388624 | tf_op jit(solution)/shard_map/all_gather | solution.py:69
  787.9 23.4 scatter_custom_fusion
  835.5 29.1 %all-gather.17.cloned.1.call-done = bf16[2048,3,1024]{2,0,1:T(8,128)(2,1)} async-done(((bf16[512,3,1024]{2,0,1:T(8,128)(2,1)}), bf16[2048,3,1024]{2,0,1:T(8,128)(2,1)}) %all-gather.17.cloned.1.call-update) | async-done | bytes 12582928 | tf_op jit(solution)/shard_map/all_gather | solution.py:183
  876.4 68.4 %all-to-all-done = bf16[24,53,2048]{2,1,0:T(8,128)(2,1)} async-done(((bf16[24,53,2048]{2,1,0:T(8,128)(2,1)}), bf16[24,53,2048]{2,1,0:T(8,128)(2,1)}, u32[]{:S(2)}, u32[]{:S(2)}) %all-to-all-start) | async-done | bytes 5210144 | tf_op jit(solution)/shard_map/all_to_all | solution.py:158
  957.2 63.6 %all-gather.15.cloned.1.call-done = bf16[2048,3,2048]{2,0,1:T(8,128)(2,1)} async-done(((bf16[512,3,2048]{2,0,1:T(8,128)(2,1)}), bf16[2048,3,2048]{2,0,1:T(8,128)(2,1)}) %all-gather.15.cloned.1.call-update) | async-done | bytes 25165840 | tf_op jit(solution)/shard_map/all_gather | solution.py:173
  1032.4 15.5 multiply_convert_fusion.1
  1087.0 15.7 add_convert_fusion
  1112.5 115.3 %all-to-all-done.1 = bf16[3,424,2048]{2,0,1:T(4,128)(2,1)} async-done(((bf16[3,424,2048]{2,0,1:T(4,128)(2,1)}), bf16[3,424,2048]{2,0,1:T(4,128)(2,1)}, u32[]{:S(2)}, u32[]{:S(2)}) %all-to-all-start.1) | async-done | bytes 5210144 | tf_op jit(solution)/shard_map/all_to_all | solution.py:216
  1249.2 135.3 %all-to-all-done.3 = bf16[3,424,2048]{2,0,1:T(4,128)(2,1)} async-done(((bf16[3,424,2048]{2,0,1:T(4,128)(2,1)}), bf16[3,424,2048]{2,0,1:T(4,128)(2,1)}, u32[]{:S(2)}, u32[]{:S(2)}) %all-to-all-start.3) | async-done | bytes 5210144 | tf_op jit(solution)/shard_map/all_to_all | solution.py:217
  1473.1 14.0 reduce-scatter.19.cloned.1.call-done
  1502.5 19.3 reduce-scatter.13.cloned.1.call-done
  1521.8 12.8 convolution_convert_fusion
  1534.7 22.9 pad_maximum_fusion.1
  1592.9 14.8 fusion.33
  1609.2 27.5 %pad_maximum_fusion = bf16[2048,3,3072]{0,2,1:T(8,128)(2,1)} fusion(bf16[2048,3,1024]{0,2,1:T(8,128)(2,1)} %convert_bitcast_fusion, bf16[2048,3,1024]{0,2,1:T(8,128)(2,1)} %convert_bitcast_fusion.1, bf16[2048,3,1024]{0,2,1:T(8,128)(2,1)} %convert_bitcast_fusion.2), kind=kLoop, calls=%fused_computation.5 | loop fusion | flops 113246208 | bytes 75497472 | tf_op jit(solution)/shard_map/concatenate | solution.py:203
  1636.8 463.8 %reduce-scatter.15.cloned.1.call-done = bf16[256,4,2048]{2,0,1:T(8,128)(2,1)} async-done(((bf16[2048,4,2048]{2,0,1:T(8,128)(2,1)}), bf16[256,4,2048]{2,0,1:T(8,128)(2,1)}) %reduce-scatter.15.cloned.1.call-update) | async-done | bytes 4194320 | tf_op jit(solution)/shard_map/reduce_scatter | solution.py:286
  2101.9 62.9 %reduce-scatter.23.cloned.1.call-done = f32[16,2]{1,0:T(8,128)} async-done(((f32[128,2]{1,0:T(8,128)}), f32[16,2]{1,0:T(8,128)}) %reduce-scatter.23.cloned.1.call-update) | async-done | bytes 144
  2165.6 65.7 %reduce-scatter.21.cloned.1.call-done = f32[256,2]{1,0:T(8,128)} async-done(((f32[2048,2]{1,0:T(8,128)}), f32[256,2]{1,0:T(8,128)}) %reduce-scatter.21.cloned.1.call-update) | async-done | bytes 2064
  2239.1 255.4 %reduce-scatter.17.cloned.1.call-done = bf16[512,3,3072]{0,2,1:T(8,128)(2,1)} async-done(((bf16[2048,3,3072]{0,2,1:T(8,128)(2,1)}), bf16[512,3,3072]{0,2,1:T(8,128)(2,1)}) %reduce-scatter.17.cloned.1.call-update) | async-done | bytes 9437200 | tf_op jit(solution)/shard_map/reduce_scatter | solution.py:202
  2515.8 12.8 copy.205
  2528.6 53.8 %all-reduce.7.cloned.1.call-done = bf16[256,4,2048]{2,0,1:T(8,128)(2,1)} async-done(((bf16[256,4,2048]{2,0,1:T(8,128)(2,1)}), bf16[256,4,2048]{2,0,1:T(8,128)(2,1)}) %all-reduce.7.cloned.1.call-update) | async-done | bytes 4194320 | tf_op jit(solution)/shard_map/psum | solution.py:299
  (312 shorter events, 382.3 us)
Async XLA Ops:
  7.2 485.6 %all-gather.9.cloned.1.call-start = ((), (), s32[]{:S(2)}) async-start(), calls=%async_computation.10 | async-start | bytes 28311552 | tf_op jit(solution)/shard_map/all_gather | solution.py:68
  7.9 555.2 %all-gather.19.cloned.1.call-start = ((), (), s32[]{:S(2)}) async-start(), calls=%async_computation.19 | async-start | bytes 2621440 | tf_op jit(solution)/shard_map/all_gather | solution.py:92
  60.5 442.6 %copy-start.47 = (f32[128]{0:T(128)}, f32[128]{0:T(128)S(1)}, u32[]{:S(2)}) copy-start(f32[128]{0:T(128)S(1)} %fusion.58) | copy-start | bytes 1540
  60.5 442.6 %copy-start.31 = (f32[2048,1]{0,1:T(1,128)}, f32[2048,1]{0,1:T(1,128)S(1)}, u32[]{:S(2)}) copy-start(f32[2048,1]{0,1:T(1,128)S(1)} %get-tuple-element.161) | copy-start | bytes 24580
  60.5 726.4 %copy-start.33 = (f32[2048,1]{0,1:T(1,128)}, f32[2048,1]{0,1:T(1,128)S(1)}, u32[]{:S(2)}) copy-start(f32[2048,1]{0,1:T(1,128)S(1)} %get-tuple-element.160) | copy-start | bytes 24580
  504.0 63.0 %all-gather.11.cloned.1.call-start = ((), (), s32[]{:S(2)}) async-start(), calls=%async_computation.11 | async-start | bytes 2621440 | tf_op jit(solution)/shard_map/all_gather | solution.py:91
  531.0 251.0 %all-gather.13.cloned.1.call-start = ((), (), s32[]{:S(2)}) async-start(), calls=%async_computation.12 | async-start | bytes 9437184 | tf_op jit(solution)/shard_map/all_gather | solution.py:69
  531.6 332.9 %all-gather.17.cloned.1.call-start = ((), (), s32[]{:S(2)}) async-start(), calls=%async_computation.14 | async-start | bytes 15728640 | tf_op jit(solution)/shard_map/all_gather | solution.py:183
  532.2 488.6 %all-gather.15.cloned.1.call-start = ((), (), s32[]{:S(2)}) async-start(), calls=%async_computation.13 | async-start | bytes 31457280 | tf_op jit(solution)/shard_map/all_gather | solution.py:173
  557.6 260.7 %all-to-all-start.2 = ((bf16[24,53,2048]{2,1,0:T(8,128)(2,1)}), bf16[24,53,2048]{2,1,0:T(8,128)(2,1)}, u32[]{:S(2)}, u32[]{:S(2)}) async-start(bf16[24,53,2048]{2,1,0:T(8,128)(2,1)} %reshape.418), calls=%async_computation.2 | async-start | bytes 11010048 | tf_op jit(solution)/shard_map/all_to_all | solution.py:165
  571.2 215.6 %copy-start.43 = (f32[16,128]{1,0:T(8,128)}, f32[16,128]{1,0:T(8,128)S(1)}, u32[]{:S(2)}) copy-start(f32[16,128]{1,0:T(8,128)S(1)} %log_add_fusion) | copy-start | bytes 24580
  575.0 211.8 %copy-start.13 = (bf16[128,16,128]{0,2,1:T(8,128)(2,1)}, bf16[128,16,128]{0,2,1:T(8,128)(2,1)S(1)}, u32[]{:S(2)}) copy-start(bf16[128,16,128]{0,2,1:T(8,128)(2,1)S(1)} %get-tuple-element.168) | copy-start | bytes 1572868
  818.3 126.5 %all-to-all-start = ((bf16[24,53,2048]{2,1,0:T(8,128)(2,1)}), bf16[24,53,2048]{2,1,0:T(8,128)(2,1)}, u32[]{:S(2)}, u32[]{:S(2)}) async-start(bf16[24,53,2048]{2,1,0:T(8,128)(2,1)} %reshape.416), calls=%async_computation | async-start | bytes 11010048 | tf_op jit(solution)/shard_map/all_to_all | solution.py:158
  1069.7 158.2 %all-to-all-start.1 = ((bf16[3,424,2048]{2,0,1:T(4,128)(2,1)}), bf16[3,424,2048]{2,0,1:T(4,128)(2,1)}, u32[]{:S(2)}, u32[]{:S(2)}) async-start(bf16[3,424,2048]{2,0,1:T(4,128)(2,1)} %copy.180), calls=%async_computation.1 | async-start | bytes 13893632 | tf_op jit(solution)/shard_map/all_to_all | solution.py:216
  1227.9 156.7 %all-to-all-start.3 = ((bf16[3,424,2048]{2,0,1:T(4,128)(2,1)}), bf16[3,424,2048]{2,0,1:T(4,128)(2,1)}, u32[]{:S(2)}, u32[]{:S(2)}) async-start(bf16[3,424,2048]{2,0,1:T(4,128)(2,1)} %copy.185), calls=%async_computation.3 | async-start | bytes 13893632 | tf_op jit(solution)/shard_map/all_to_all | solution.py:217
  1232.8 254.3 %reduce-scatter.19.cloned.1.call-start = ((), (), s32[]{:S(2)}) async-start(), calls=%async_computation.20 | async-start | bytes 2621440
  1457.4 64.4 %reduce-scatter.13.cloned.1.call-start = ((), (), s32[]{:S(2)}) async-start(), calls=%async_computation.15 | async-start | bytes 2621440 | tf_op jit(solution)/shard_map/reduce_scatter | solution.py:270
  1466.5 634.1 %reduce-scatter.15.cloned.1.call-start = ((), (), s32[]{:S(2)}) async-start(), calls=%async_computation.16 | async-start | bytes 37748736 | tf_op jit(solution)/shard_map/reduce_scatter | solution.py:286
  1557.5 607.3 %reduce-scatter.23.cloned.1.call-start = ((), (), s32[]{:S(2)}) async-start(), calls=%async_computation.22 | async-start | bytes 73728
  1592.8 638.5 %reduce-scatter.21.cloned.1.call-start = ((), (), s32[]{:S(2)}) async-start(), calls=%async_computation.21 | async-start | bytes 1179648
  1609.1 885.4 %reduce-scatter.17.cloned.1.call-start = ((), (), s32[]{:S(2)}) async-start(), calls=%async_computation.18 | async-start | bytes 47185920 | tf_op jit(solution)/shard_map/reduce_scatter | solution.py:202
  1636.7 463.9 %copy-start.59 = (f32[128]{0:T(128)S(1)}, f32[128]{0:T(128)}, u32[]{:S(2)}) copy-start(f32[128]{0:T(128)} %copy-done.58) | copy-start | bytes 1540
  1636.7 464.0 %copy-start.25 = (f32[128,2048]{1,0:T(8,128)S(1)}, f32[128,2048]{1,0:T(8,128)}, u32[]{:S(2)}) copy-start(f32[128,2048]{1,0:T(8,128)} %get-tuple-element.172) | copy-start | bytes 3145732
  1636.8 945.7 %all-reduce.7.cloned.1.call-start = ((), (), s32[]{:S(2)}) async-start(), calls=%async_computation.17 | async-start | bytes 8388608 | tf_op jit(solution)/shard_map/psum | solution.py:299
  (61 other events, 815.2 us)
Sparse Core Ops, SparseCore 0:
  9.5 483.2 all-gather.8
  504.1 22.5 all-gather.18
  531.1 20.5 all-gather.10
  553.7 228.2 all-gather.12
  783.4 81.0 all-gather.16
  866.0 154.8 all-gather.14
  1457.5 29.5 reduce-scatter.18
  1490.3 31.4 reduce-scatter.12
  1557.7 542.9 reduce-scatter.14
  2104.4 60.3 reduce-scatter.22
  2168.8 62.4 reduce-scatter.20
  2234.0 260.5 reduce-scatter.16
  2496.9 85.5 all-reduce.6
where the time goes:
time: 2610 us; the launch traced here: 2600 us
  waiting for transfers between devices  1990 us (76%)
  local copies, waits for them, and re-layouts  213 us (8%)
  matrix products  184 us (7%)
  other arithmetic  102 us (4%)
  blocking collectives  75.5 us (3%)
    reduce_scatter x1, waiting for transfers between devices, body(): lax.psum_scatter(jnp.concatenate([projections, output_part[:, None, :]],...  464 us
    all_gather x1, waiting for transfers between devices, body(): lax.all_gather(qkv_w, 'fsdp', axis=0, tiled=True)  432 us
    reduce_scatter x1, waiting for transfers between devices, body(): lax.psum_scatter(jnp.concatenate([jnp.einsum('erd,erk->dek', got_rows, ga...  255 us
    all_gather x1, waiting for transfers between devices, body(): lax.all_gather(out_w, 'fsdp', axis=0, tiled=True)  207 us
    unnamed x16, waiting for transfers between devices  145 us
    all_to_all x1, waiting for transfers between devices, body(): lax.all_to_all(input_grads, 'fsdp', split_axis=1, concat_axis=0, tiled=True)  135 us
    all_to_all x1, waiting for transfers between devices, body(): lax.all_to_all(made_rows, 'fsdp', split_axis=1, concat_axis=0, tiled=True)  115 us
    all_to_all x1, waiting for transfers between devices, body(): lax.all_to_all(send_rows.reshape(experts_all, capacity, model_width), 'fs...  68.4 us
  transfers between devices with their start and end apart: 17, of which 14 were waited for; matrix products, arithmetic and copies ran while one was open for 12% of the time, Pallas kernels for 0%

commit v1 on v0

--- a/solution.py
+++ b/solution.py
@@ -170,7 +170,12 @@
             tiled=True,
         ),
     )
-    segment = lax.all_gather(gate_up, "ctx", axis=0, tiled=True)
+    ring = [gate_up]
+    for hop in range(3):
+        ring.append(lax.ppermute(ring[-1], "ctx", [(dev, (dev + 1) % 4) for dev in range(4)]))
+    segment = jnp.roll(
+        jnp.concatenate(ring[::-1], axis=0), (lax.axis_index("ctx") + 1) * ring[0].shape[0], axis=0
+    )
     gate_add = jnp.einsum(
         "erd,dek->erk", got_rows, segment[:, :, :hidden_units], preferred_element_type=f32
     )

time: 2610 us -> 2560 us (0.981)
  waiting for transfers between devices: 1990 us -> 1880 us
  local copies, waits for them, and re-layouts: 213 us -> 264 us
    all_gather x1, waiting for transfers between devices: 207 us -> 29.9 us  [body(): lax.all_gather(out_w, 'fsdp', axis=0, tiled=True)]
    ppermute x0 -> x3, waiting for transfers between devices: none -> 122 us  [body(): lax.ppermute(ring[-1], 'ctx', [(dev, (dev + 1) % 4) for dev in range(4)])]
    unnamed x155 -> x164, local copies, waits for them, and re-layouts: 44.9 us -> 92.9 us
    all_to_all x1, waiting for transfers between devices: 0.01 us -> 35.5 us  [body(): lax.all_to_all(send_grads.reshape(experts_all, capacity, model_width), 'f...]
    all_gather x1, waiting for transfers between devices: 63.6 us -> 28.9 us  [body(): segment = lax.all_gather(gate_up, 'ctx', axis=0, tiled=True)]
    all_gather x1, waiting for transfers between devices: 29.1 us -> 0.01 us  [body(): segment = lax.all_gather(down_t, 'ctx', axis=0, tiled=True)]
  transfers between devices with their start and end apart: 17 -> 20, of which waited for: 14 -> 16; matrix products, arithmetic and copies ran while one was open for 12% -> 15% of each run, Pallas kernels for 0% -> 0%
where the time goes in v1:
time: 2560 us; the launch traced here: 2550 us
  waiting for transfers between devices  1880 us (73%)
  local copies, waits for them, and re-layouts  264 us (10%)
  matrix products  188 us (7%)
  other arithmetic  101 us (4%)
  blocking collectives  75.5 us (3%)
    reduce_scatter x1, waiting for transfers between devices, body(): lax.psum_scatter(jnp.concatenate([projections, output_part[:, None, :]],...  465 us
    all_gather x1, waiting for transfers between devices, body(): lax.all_gather(qkv_w, 'fsdp', axis=0, tiled=True)  432 us
    reduce_scatter x1, waiting for transfers between devices, body(): lax.psum_scatter(jnp.concatenate([jnp.einsum('erd,erk->dek', got_rows, ga...  255 us
    unnamed x16, waiting for transfers between devices  144 us
    all_to_all x1, waiting for transfers between devices, body(): lax.all_to_all(input_grads, 'fsdp', split_axis=1, concat_axis=0, tiled=True)  129 us
    ppermute x3, waiting for transfers between devices, body(): lax.ppermute(ring[-1], 'ctx', [(dev, (dev + 1) % 4) for dev in range(4)])  122 us
    all_to_all x1, waiting for transfers between devices, body(): lax.all_to_all(made_rows, 'fsdp', split_axis=1, concat_axis=0, tiled=True)  118 us
    unnamed x164, local copies, waits for them, and re-layouts  92.9 us
  transfers between devices with their start and end apart: 20, of which 16 were waited for; matrix products, arithmetic and copies ran while one was open for 15% of the time, Pallas kernels for 0%

profile of v1, /device:TPU:0, one launch (start us, length us, event | category | flops | bytes accessed | tf_op | source)
XLA Modules:
  0.0 2548.2 jit_solution(13914272970009343476)
XLA Ops:
  7.9 50.7 %all_gather.24 = bf16[2048,2]{0,1:T(2,128)(2,1)S(1)} all-gather(bf16[256,2]{0,1:T(2,128)(2,1)} %param.17), channel_id=1, replica_groups=mesh['ctx'=4,'fsdp'=8] {'fsdp'}, dimensions={0}, use_global_device_ids=true | all-gather | bytes 9216 | tf_op jit(solution)/shard_map/all_gather | solution.py:70
  60.4 432.4 %all-gather.9.cloned.1.call-done = bf16[2048,3,2048]{2,0,1:T(8,128)(2,1)} async-done(((bf16[256,3,2048]{2,0,1:T(8,128)(2,1)}), bf16[2048,3,2048]{2,0,1:T(8,128)(2,1)}) %all-gather.9.cloned.1.call-update) | async-done | bytes 25165840 | tf_op jit(solution)/shard_map/all_gather | solution.py:68
  504.1 19.2 all-gather.1
  541.0 73.9 %collective-permute-done = bf16[512,3,2048]{2,0,1:T(8,128)(2,1)} collective-permute-done((bf16[512,3,2048]{2,0,1:T(8,128)(2,1)}, bf16[512,3,2048]{2,0,1:T(8,128)(2,1)}, u32[]{:S(2)}, u32[]{:S(2)}) %collective-permute-start) | collective-permute-done | bytes 6291488 | tf_op jit(solution)/shard_map/ppermute | solution.py:175
  637.4 48.6 %collective-permute-done.1 = bf16[512,3,2048]{2,0,1:T(8,128)(2,1)} collective-permute-done((bf16[512,3,2048]{2,0,1:T(8,128)(2,1)}, bf16[512,3,2048]{2,0,1:T(8,128)(2,1)}, u32[]{:S(2)}, u32[]{:S(2)}) %collective-permute-start.1) | collective-permute-done | bytes 6291488 | tf_op jit(solution)/shard_map/ppermute | solution.py:175
  697.6 29.9 %all-gather.13.cloned.1.call-done = bf16[2048,2048]{1,0:T(8,128)(2,1)} async-done(((bf16[256,2048]{1,0:T(8,128)(2,1)}), bf16[2048,2048]{1,0:T(8,128)(2,1)}) %all-gather.13.cloned.1.call-update) | async-done | bytes 8388624 | tf_op jit(solution)/shard_map/all_gather | solution.py:69
  733.4 23.3 scatter_custom_fusion
  763.6 35.5 %all-to-all-done.2 = bf16[24,53,2048]{2,1,0:T(8,128)(2,1)} async-done(((bf16[24,53,2048]{2,1,0:T(8,128)(2,1)}), bf16[24,53,2048]{2,1,0:T(8,128)(2,1)}, u32[]{:S(2)}, u32[]{:S(2)}) %all-to-all-start.2) | async-done | bytes 5210144 | tf_op jit(solution)/shard_map/all_to_all | solution.py:165
  878.3 47.3 %all-to-all-done = bf16[24,53,2048]{2,1,0:T(8,128)(2,1)} async-done(((bf16[24,53,2048]{2,1,0:T(8,128)(2,1)}), bf16[24,53,2048]{2,1,0:T(8,128)(2,1)}, u32[]{:S(2)}, u32[]{:S(2)}) %all-to-all-start) | async-done | bytes 5210144 | tf_op jit(solution)/shard_map/all_to_all | solution.py:158
  949.7 15.7 multiply_convert_fusion.1
  965.4 28.9 %all-gather.17.cloned.1.call-done = bf16[2048,3,2048]{2,0,1:T(8,128)(2,1)} async-done(((bf16[512,3,2048]{2,0,1:T(8,128)(2,1)}), bf16[2048,3,2048]{2,0,1:T(8,128)(2,1)}) %all-gather.17.cloned.1.call-update) | async-done | bytes 25165840 | tf_op jit(solution)/shard_map/all_gather | solution.py:199
  1006.0 15.7 add_convert_fusion
  1037.9 14.0 convolution_convert_fusion.1
  1061.7 128.8 %all-to-all-done.3 = bf16[3,424,2048]{2,0,1:T(4,128)(2,1)} async-done(((bf16[3,424,2048]{2,0,1:T(4,128)(2,1)}), bf16[3,424,2048]{2,0,1:T(4,128)(2,1)}, u32[]{:S(2)}, u32[]{:S(2)}) %all-to-all-start.3) | async-done | bytes 5210144 | tf_op jit(solution)/shard_map/all_to_all | solution.py:222
  1228.9 118.2 %all-to-all-done.1 = bf16[3,424,2048]{2,0,1:T(4,128)(2,1)} async-done(((bf16[3,424,2048]{2,0,1:T(4,128)(2,1)}), bf16[3,424,2048]{2,0,1:T(4,128)(2,1)}, u32[]{:S(2)}, u32[]{:S(2)}) %all-to-all-start.1) | async-done | bytes 5210144 | tf_op jit(solution)/shard_map/all_to_all | solution.py:221
  1451.4 19.4 reduce-scatter.13.cloned.1.call-done
  1483.6 22.9 pad_maximum_fusion.1
  1542.4 14.7 fusion.33
  1558.5 26.5 %pad_maximum_fusion = bf16[2048,3,3072]{0,2,1:T(8,128)(2,1)} fusion(bf16[2048,3,1024]{0,2,1:T(8,128)(2,1)} %convert_bitcast_fusion, bf16[2048,3,1024]{0,2,1:T(8,128)(2,1)} %convert_bitcast_fusion.1, bf16[2048,3,1024]{0,2,1:T(8,128)(2,1)} %convert_bitcast_fusion.2), kind=kLoop, calls=%fused_computation.5 | loop fusion | flops 113246208 | bytes 75497472 | tf_op jit(solution)/shard_map/concatenate | solution.py:208
  1585.1 465.0 %reduce-scatter.15.cloned.1.call-done = bf16[256,4,2048]{2,0,1:T(8,128)(2,1)} async-done(((bf16[2048,4,2048]{2,0,1:T(8,128)(2,1)}), bf16[256,4,2048]{2,0,1:T(8,128)(2,1)}) %reduce-scatter.15.cloned.1.call-update) | async-done | bytes 4194320 | tf_op jit(solution)/shard_map/reduce_scatter | solution.py:291
  2051.4 62.8 %reduce-scatter.23.cloned.1.call-done = f32[16,2]{1,0:T(8,128)} async-done(((f32[128,2]{1,0:T(8,128)}), f32[16,2]{1,0:T(8,128)}) %reduce-scatter.23.cloned.1.call-update) | async-done | bytes 144
  2115.0 65.6 %reduce-scatter.21.cloned.1.call-done = f32[256,2]{1,0:T(8,128)} async-done(((f32[2048,2]{1,0:T(8,128)}), f32[256,2]{1,0:T(8,128)}) %reduce-scatter.21.cloned.1.call-update) | async-done | bytes 2064
  2188.4 255.4 %reduce-scatter.17.cloned.1.call-done = bf16[512,3,3072]{0,2,1:T(8,128)(2,1)} async-done(((bf16[2048,3,3072]{0,2,1:T(8,128)(2,1)}), bf16[512,3,3072]{0,2,1:T(8,128)(2,1)}) %reduce-scatter.17.cloned.1.call-update) | async-done | bytes 9437200 | tf_op jit(solution)/shard_map/reduce_scatter | solution.py:207
  2478.3 53.4 %all-reduce.7.cloned.1.call-done = bf16[256,4,2048]{2,0,1:T(8,128)(2,1)} async-done(((bf16[256,4,2048]{2,0,1:T(8,128)(2,1)}), bf16[256,4,2048]{2,0,1:T(8,128)(2,1)}) %all-reduce.7.cloned.1.call-update) | async-done | bytes 4194320 | tf_op jit(solution)/shard_map/psum | solution.py:304
  (328 shorter events, 465.3 us)
Async XLA Ops:
  7.2 485.6 %all-gather.9.cloned.1.call-start = ((), (), s32[]{:S(2)}) async-start(), calls=%async_computation.10 | async-start | bytes 28311552 | tf_op jit(solution)/shard_map/all_gather | solution.py:68
  7.9 678.1 %all-gather.19.cloned.1.call-start = ((), (), s32[]{:S(2)}) async-start(), calls=%async_computation.19 | async-start | bytes 2621440 | tf_op jit(solution)/shard_map/all_gather | solution.py:92
  60.4 442.7 %copy-start.47 = (f32[128]{0:T(128)}, f32[128]{0:T(128)S(1)}, u32[]{:S(2)}) copy-start(f32[128]{0:T(128)S(1)} %fusion.60) | copy-start | bytes 1540
  60.4 671.9 %copy-start.32 = (f32[2048,1]{0,1:T(1,128)}, f32[2048,1]{0,1:T(1,128)S(1)}, u32[]{:S(2)}) copy-start(f32[2048,1]{0,1:T(1,128)S(1)} %get-tuple-element.160) | copy-start | bytes 24580
  504.0 185.5 %all-gather.11.cloned.1.call-start = ((), (), s32[]{:S(2)}) async-start(), calls=%async_computation.11 | async-start | bytes 2621440 | tf_op jit(solution)/shard_map/all_gather | solution.py:91
  531.1 196.4 %all-gather.13.cloned.1.call-start = ((), (), s32[]{:S(2)}) async-start(), calls=%async_computation.12 | async-start | bytes 9437184 | tf_op jit(solution)/shard_map/all_gather | solution.py:69
  531.7 335.1 %all-gather.15.cloned.1.call-start = ((), (), s32[]{:S(2)}) async-start(), calls=%async_computation.13 | async-start | bytes 15728640 | tf_op jit(solution)/shard_map/all_gather | solution.py:188
  532.3 462.0 %all-gather.17.cloned.1.call-start = ((), (), s32[]{:S(2)}) async-start(), calls=%async_computation.14 | async-start | bytes 31457280 | tf_op jit(solution)/shard_map/all_gather | solution.py:199
  532.8 82.0 %collective-permute-start = (bf16[512,3,2048]{2,0,1:T(8,128)(2,1)}, bf16[512,3,2048]{2,0,1:T(8,128)(2,1)}, u32[]{:S(2)}, u32[]{:S(2)}) collective-permute-start(bf16[512,3,2048]{2,0,1:T(8,128)(2,1)} %param.19), channel_id=1, source_target_pairs={{0,8},{8,16},{16,24},{24,0},{1,9},{9,17},{17,25},{25,1},{2,10},{10... | collective-permute-start | bytes 18874376 | tf_op jit(solution)/shard_map/ppermute | solution.py:175
  614.8 71.2 %collective-permute-start.1 = (bf16[512,3,2048]{2,0,1:T(8,128)(2,1)}, bf16[512,3,2048]{2,0,1:T(8,128)(2,1)}, u32[]{:S(2)}, u32[]{:S(2)}) collective-permute-start(bf16[512,3,2048]{2,0,1:T(8,128)(2,1)} %collective-permute-done), channel_id=1, source_target_pairs={{0,8},{8,16},{16,24},{24,0},{1,9},{9,17},{17,25},{25,1},{2,10},{10... | collective-permute-start | bytes 18874376 | tf_op jit(solution)/shard_map/ppermute | solution.py:175
  631.9 167.2 %all-to-all-start.2 = ((bf16[24,53,2048]{2,1,0:T(8,128)(2,1)}), bf16[24,53,2048]{2,1,0:T(8,128)(2,1)}, u32[]{:S(2)}, u32[]{:S(2)}) async-start(bf16[24,53,2048]{2,1,0:T(8,128)(2,1)} %reshape.418), calls=%async_computation.2 | async-start | bytes 11010048 | tf_op jit(solution)/shard_map/all_to_all | solution.py:165
  686.0 130.2 %collective-permute-start.2 = (bf16[512,3,2048]{2,0,1:T(8,128)(2,1)}, bf16[512,3,2048]{2,0,1:T(8,128)(2,1)}, u32[]{:S(2)}, u32[]{:S(2)}) collective-permute-start(bf16[512,3,2048]{2,0,1:T(8,128)(2,1)} %collective-permute-done.1), channel_id=1, source_target_pairs={{0,8},{8,16},{16,24},{24,0},{1,9},{9,17},{17,25},{25,1},{2,10},{10... | collective-permute-start | bytes 18874376 | tf_op jit(solution)/shard_map/ppermute | solution.py:175
  799.1 126.5 %all-to-all-start = ((bf16[24,53,2048]{2,1,0:T(8,128)(2,1)}), bf16[24,53,2048]{2,1,0:T(8,128)(2,1)}, u32[]{:S(2)}, u32[]{:S(2)}) async-start(bf16[24,53,2048]{2,1,0:T(8,128)(2,1)} %reshape.416), calls=%async_computation | async-start | bytes 11010048 | tf_op jit(solution)/shard_map/all_to_all | solution.py:158
  1031.6 158.9 %all-to-all-start.3 = ((bf16[3,424,2048]{2,0,1:T(4,128)(2,1)}), bf16[3,424,2048]{2,0,1:T(4,128)(2,1)}, u32[]{:S(2)}, u32[]{:S(2)}) async-start(bf16[3,424,2048]{2,0,1:T(4,128)(2,1)} %copy.185), calls=%async_computation.3 | async-start | bytes 13893632 | tf_op jit(solution)/shard_map/all_to_all | solution.py:222
  1190.5 156.6 %all-to-all-start.1 = ((bf16[3,424,2048]{2,0,1:T(4,128)(2,1)}), bf16[3,424,2048]{2,0,1:T(4,128)(2,1)}, u32[]{:S(2)}, u32[]{:S(2)}) async-start(bf16[3,424,2048]{2,0,1:T(4,128)(2,1)} %copy.180), calls=%async_computation.1 | async-start | bytes 13893632 | tf_op jit(solution)/shard_map/all_to_all | solution.py:221
  1195.3 240.8 %reduce-scatter.19.cloned.1.call-start = ((), (), s32[]{:S(2)}) async-start(), calls=%async_computation.20 | async-start | bytes 2621440
  1406.4 64.4 %reduce-scatter.13.cloned.1.call-start = ((), (), s32[]{:S(2)}) async-start(), calls=%async_computation.15 | async-start | bytes 2621440 | tf_op jit(solution)/shard_map/reduce_scatter | solution.py:275
  1415.5 634.5 %reduce-scatter.15.cloned.1.call-start = ((), (), s32[]{:S(2)}) async-start(), calls=%async_computation.16 | async-start | bytes 37748736 | tf_op jit(solution)/shard_map/reduce_scatter | solution.py:291
  1506.5 607.7 %reduce-scatter.23.cloned.1.call-start = ((), (), s32[]{:S(2)}) async-start(), calls=%async_computation.22 | async-start | bytes 73728
  1542.1 638.5 %reduce-scatter.21.cloned.1.call-start = ((), (), s32[]{:S(2)}) async-start(), calls=%async_computation.21 | async-start | bytes 1179648
  1558.4 885.4 %reduce-scatter.17.cloned.1.call-start = ((), (), s32[]{:S(2)}) async-start(), calls=%async_computation.18 | async-start | bytes 47185920 | tf_op jit(solution)/shard_map/reduce_scatter | solution.py:207
  1585.0 465.1 %copy-start.59 = (f32[128]{0:T(128)S(1)}, f32[128]{0:T(128)}, u32[]{:S(2)}) copy-start(f32[128]{0:T(128)} %copy-done.58) | copy-start | bytes 1540
  1585.0 465.1 %copy-start.24 = (f32[128,2048]{1,0:T(8,128)S(1)}, f32[128,2048]{1,0:T(8,128)}, u32[]{:S(2)}) copy-start(f32[128,2048]{1,0:T(8,128)} %get-tuple-element.172) | copy-start | bytes 3145732
  1585.0 946.7 %all-reduce.7.cloned.1.call-start = ((), (), s32[]{:S(2)}) async-start(), calls=%async_computation.17 | async-start | bytes 8388608 | tf_op jit(solution)/shard_map/psum | solution.py:304
  (65 other events, 1558.0 us)
Sparse Core Ops, SparseCore 0:
  9.5 483.2 all-gather.8
  504.1 22.5 all-gather.18
  531.2 26.1 all-gather.10
  559.4 168.0 all-gather.12
  728.9 109.0 all-gather.14
  839.4 154.8 all-gather.16
  1406.5 29.5 reduce-scatter.18
  1439.3 31.3 reduce-scatter.12
  1506.7 543.3 reduce-scatter.14
  2053.9 60.2 reduce-scatter.22
  2118.2 62.3 reduce-scatter.20
  2183.3 260.4 reduce-scatter.16
  2446.2 85.4 all-reduce.6
